TPU v7x, 32 devices: a whole 2x2x4 slice. The times are simulated.
32 devices in a mesh: dp: 8 (over z, x), tensor: 4 (over y, core).
Axes of the slice: x: 2, y: 2, z: 4, core: 2. Of those that a mesh axis runs over, the one named last changes fastest.
Arguments:
- tokens_in: bfloat16 [12288, 768], P('dp'), may hold values from -6 to 6
- cotangent: bfloat16 [12288, 768], P('dp'), may hold values from -6 to 6
- span_mask: int32 [12288], P('dp'), may hold values from 0 to 1, as said below
- lengths: int32 [24], P('dp'), may hold values from 128 to 512, as said below
- step: int32 [1], replicated, may hold values from 1000 to 31999
- warmup: int32 [1], replicated, may hold values from 1000 to 29999
- total: int32 [1], replicated, may hold values from 32000 to 40000
- w_qkv: float32 [768, 3, 768], P(None, None, 'tensor'), may hold values from -0.21875 to 0.21875
- w_out: float32 [768, 768], P(None, 'tensor'), may hold values from -1.25 to 1.25
- w_in: float32 [768, 3072], P(None, 'tensor'), may hold values from -0.21875 to 0.21875
- w_back: float32 [768, 3072], P(None, 'tensor'), may hold values from -0.109375 to 0.109375
- gains: float32 [2, 768], replicated, may hold values from 0.5 to 1.5
- biases: float32 [6, 768], replicated, may hold values from -3 to 3
- bias_in: float32 [3072], replicated, may hold values from -3 to 3
- mom_qkv: float32 [2, 768, 3, 768], P(None, 'dp', None, 'tensor'), as said below
- mom_out: float32 [2, 768, 768], P(None, 'dp', 'tensor'), as said below
- mom_in: float32 [2, 768, 3072], P(None, 'dp', 'tensor'), as said below
- mom_back: float32 [2, 768, 3072], P(None, 'dp', 'tensor'), as said below
- mom_gains: float32 [2, 2, 768], replicated, as said below
- mom_biases: float32 [2, 6, 768], replicated, as said below
- mom_bias_in: float32 [2, 3072], replicated, as said below
Outputs:
- normed_out: bfloat16 [12288, 768], P('dp')
- input_grad: float32 [12288, 768], P('dp')
- change_qkv: float32 [768, 3, 768], P(None, None, 'tensor')
- change_out_proj: float32 [768, 768], P(None, 'tensor')
- change_in_proj: float32 [768, 3072], P(None, 'tensor')
- change_back_proj: float32 [768, 3072], P(None, 'tensor')
- change_gains: float32 [2, 768], replicated
- change_biases: float32 [6, 768], replicated
- change_bias_in: float32 [3072], replicated
- new_mom_qkv: float32 [2, 768, 3, 768], P(None, 'dp', None, 'tensor')
- new_mom_out: float32 [2, 768, 768], P(None, 'dp', 'tensor')
- new_mom_in: float32 [2, 768, 3072], P(None, 'dp', 'tensor')
- new_mom_back: float32 [2, 768, 3072], P(None, 'dp', 'tensor')
- new_mom_gains: float32 [2, 2, 768], replicated
- new_mom_biases: float32 [2, 6, 768], replicated
- new_mom_bias_in: float32 [2, 3072], replicated
Inputs may be any that keep to these rules, and one draw needn't show every extreme that they name: `span_mask`: marked positions lie below their sequence's length and form unions of spans of 1 to 10 positions; each sequence has at most 76 of them, and in every draw each of the 3 sequences of some index of dp has exactly 76. `lengths`: a sequence's real tokens stand at its start, the rest is padding. step < total. warmup < total. `mom_qkv`: index 1 of the leading dimension holds positive second moments. `mom_out`: index 1 of the leading dimension holds positive second moments. `mom_in`: index 1 of the leading dimension holds positive second moments. `mom_back`: index 1 of the leading dimension holds positive second moments. `mom_gains`: index 1 of the leading dimension holds positive second moments. `mom_biases`: index 1 of the leading dimension holds positive second moments. `mom_bias_in`: index 1 of the leading dimension holds positive second moments.
All inputs are finite; a program needn't handle non-finite values.
Results may differ from a plain program's by a relative error of at most 0.017.
The roundings to bfloat16 on the way count: a program that leaves them out, or rounds other values in their place, can miss the bound.
Values sent between devices are 32-bit elements; how exact they have to be, the bound alone decides.
A program may use at most 128 MiB of HBM per device.

v0:
```python
import math
import jax
import jax.numpy as jnp
from jax import lax
from jax.sharding import PartitionSpec as P

HD = 64
SPAN_ROWS = 80
NORM_EPS = 1e-12
BETA_ONE = 0.9
BETA_TWO = 0.999
ADAM_EPS = 1e-06
WEIGHT_DECAY = 0.01


def layer_norm(values, gain, shift):
    center = values - jnp.mean(values, axis=-1, keepdims=True)
    spread = jnp.mean(center * center, axis=-1, keepdims=True)
    return center * lax.rsqrt(spread + NORM_EPS) * gain + shift


def exact_gelu(values):
    return jax.nn.gelu(values, approximate=False)


def outer_sum(left, right):
    return jnp.einsum("ta,tb->ab", left, right, preferred_element_type=jnp.float32)


def adam_step(weight, grad, moments, ratio, corr_one, corr_two, decay):
    first = BETA_ONE * moments[0] + (1.0 - BETA_ONE) * grad
    second = BETA_TWO * moments[1] + (1.0 - BETA_TWO) * grad * grad
    update = first / corr_one / (jnp.sqrt(second / corr_two) + ADAM_EPS) + decay * weight
    return (-ratio * update, jnp.stack([first, second]))


def on_device(
    tokens_in,
    cotangent,
    span_mask,
    lengths,
    step,
    warmup,
    total,
    w_qkv,
    w_out,
    w_in,
    w_back,
    gains,
    biases,
    bias_in,
    mom_qkv,
    mom_out,
    mom_in,
    mom_back,
    mom_gains,
    mom_biases,
    mom_bias_in,
):
    row_count, model_width = tokens_in.shape
    seq_count = lengths.shape[0]
    seq_length = row_count // seq_count
    head_cols = w_qkv.shape[2]
    hidden_cols = w_in.shape[1]
    head_size = HD
    local_heads = head_cols // head_size
    query_scale = 1.0 / math.sqrt(head_size)
    tensor_slot = lax.axis_index("tensor")
    bias_query = lax.dynamic_slice_in_dim(biases[0], tensor_slot * head_cols, head_cols)
    bias_value = lax.dynamic_slice_in_dim(biases[1], tensor_slot * head_cols, head_cols)
    bias_hidden = lax.dynamic_slice_in_dim(bias_in, tensor_slot * hidden_cols, hidden_cols)
    qkv_low = w_qkv.astype(jnp.bfloat16).reshape(model_width, 3 * head_cols)
    out_low = w_out.astype(jnp.bfloat16)
    in_low = w_in.astype(jnp.bfloat16)
    down_low = w_back.astype(jnp.bfloat16)
    projected = jnp.dot(tokens_in, qkv_low, preferred_element_type=jnp.float32).reshape(
        row_count, 3, head_cols
    )
    attn_shape = (seq_count, seq_length, local_heads, head_size)
    queries = (
        ((projected[:, 0] + bias_query) * query_scale).astype(jnp.bfloat16).reshape(attn_shape)
    )
    keys = projected[:, 1].astype(jnp.bfloat16).reshape(attn_shape)
    values = (projected[:, 2] + bias_value).astype(jnp.bfloat16).reshape(attn_shape)
    positions = jnp.arange(seq_length, dtype=jnp.int32)
    inside = positions[None, :] < lengths[:, None]
    key_bias = jnp.where(inside, 0.0, -1000000000.0).astype(jnp.float32)

    def score_block():
        raw = jnp.einsum("sqhd,skhd->shqk", queries, keys, preferred_element_type=jnp.float32)
        return raw + key_bias[:, None, None, :]

    scores = score_block()
    peak = jnp.max(scores, axis=-1, keepdims=True)
    log_total = peak + jnp.log(jnp.sum(jnp.exp(scores - peak), axis=-1, keepdims=True))
    probs_low = jnp.exp(scores - log_total).astype(jnp.bfloat16)
    context_low = (
        jnp.einsum("shqk,skhd->sqhd", probs_low, values, preferred_element_type=jnp.float32)
        .reshape(row_count, head_cols)
        .astype(jnp.bfloat16)
    )
    attn_part = jnp.einsum("tc,dc->td", context_low, out_low, preferred_element_type=jnp.float32)
    attn_sum = lax.psum(attn_part, "tensor")
    residual_one = tokens_in.astype(jnp.float32) + attn_sum + biases[2]
    normed = layer_norm(residual_one, gains[0], biases[3])
    normed_low = normed.astype(jnp.bfloat16)
    pre_act = jnp.dot(normed_low, in_low, preferred_element_type=jnp.float32) + bias_hidden
    act_low = exact_gelu(pre_act).astype(jnp.bfloat16)
    down_part = jnp.einsum("tf,df->td", act_low, down_low, preferred_element_type=jnp.float32)
    down_sum = lax.psum(down_part, "tensor")
    residual_two = normed + down_sum + biases[4]
    live = inside.astype(jnp.int32) * span_mask.reshape(seq_count, seq_length) > 0
    upto = (positions[:, None] <= positions[None, :]).astype(jnp.float32)
    rank = jnp.dot(live.astype(jnp.float32), upto).astype(jnp.int32) - 1
    slots = jnp.arange(SPAN_ROWS, dtype=jnp.int32)
    pick = (live[:, None, :] & (rank[:, None, :] == slots[None, :, None])).astype(jnp.float32)
    pick_low = pick.astype(jnp.bfloat16)

    def rows_of(values):
        width = values.shape[-1]
        return jnp.einsum(
            "srt,std->srd",
            pick,
            values.reshape(seq_count, seq_length, width),
            precision=lax.Precision.HIGHEST,
        ).reshape(seq_count * SPAN_ROWS, width)

    def low_rows_of(values):
        width = values.shape[-1]
        return jnp.einsum(
            "srt,std->srd",
            pick_low,
            values.reshape(seq_count, seq_length, width),
            preferred_element_type=jnp.bfloat16,
        ).reshape(seq_count * SPAN_ROWS, width)

    result = layer_norm(residual_two, gains[1], biases[5])
    normed_out = result.astype(jnp.bfloat16)
    residual_one_rows = rows_of(residual_one)
    residual_two_rows = rows_of(residual_two)
    grad_result = low_rows_of(cotangent).astype(jnp.float32)
    _, norm_two_back = jax.vjp(layer_norm, residual_two_rows, gains[1], biases[5])
    d_res_two, d_gain_two, d_shift_two = norm_two_back(grad_result)
    d_res_two_low = d_res_two.astype(jnp.bfloat16)
    normed_low_rows = low_rows_of(normed_low)
    pre_rows = jnp.dot(normed_low_rows, in_low, preferred_element_type=jnp.float32) + bias_hidden
    act_rows, gelu_back = jax.vjp(exact_gelu, pre_rows)
    grad_back = outer_sum(d_res_two_low, act_rows.astype(jnp.bfloat16))
    d_act = jnp.dot(d_res_two_low, down_low, preferred_element_type=jnp.float32)
    d_pre = gelu_back(d_act)[0]
    d_pre_low = d_pre.astype(jnp.bfloat16)
    grad_in = outer_sum(normed_low_rows, d_pre_low)
    d_normed_part = jnp.einsum("tf,df->td", d_pre_low, in_low, preferred_element_type=jnp.float32)
    d_normed = lax.psum(d_normed_part, "tensor") + d_res_two
    _, norm_one_back = jax.vjp(layer_norm, residual_one_rows, gains[0], biases[3])
    d_res_one, d_gain_one, d_shift_one = norm_one_back(d_normed)
    d_res_one_low = d_res_one.astype(jnp.bfloat16)
    grad_out_proj = outer_sum(d_res_one_low, low_rows_of(context_low))
    row_shape = (seq_count, SPAN_ROWS, local_heads, head_size)
    d_context = (
        jnp.dot(d_res_one_low, out_low, preferred_element_type=jnp.float32)
        .astype(jnp.bfloat16)
        .reshape(row_shape)
    )
    query_rows = low_rows_of(queries.reshape(row_count, head_cols)).reshape(row_shape)
    raw = jnp.einsum("sqhd,skhd->shqk", query_rows, keys, preferred_element_type=jnp.float32)
    probs = jax.nn.softmax(raw + key_bias[:, None, None, :], axis=-1)
    probs_again = probs.astype(jnp.bfloat16)
    d_probs = jnp.einsum("sqhd,skhd->shqk", d_context, values, preferred_element_type=jnp.float32)
    d_values = jnp.einsum(
        "shqk,sqhd->skhd", probs_again, d_context, preferred_element_type=jnp.float32
    ).reshape(row_count, head_cols)
    d_scores = (probs * (d_probs - jnp.sum(probs * d_probs, axis=-1, keepdims=True))).astype(
        jnp.bfloat16
    )
    d_queries = (
        jnp.einsum("shqk,skhd->sqhd", d_scores, keys, preferred_element_type=jnp.float32).reshape(
            seq_count * SPAN_ROWS, head_cols
        )
        * query_scale
    )
    d_keys = jnp.einsum(
        "shqk,sqhd->skhd", d_scores, query_rows, preferred_element_type=jnp.float32
    ).reshape(row_count, head_cols)

    def spread(row_values):
        width = row_values.shape[-1]
        return jnp.einsum(
            "srt,srd->std",
            pick,
            row_values.reshape(seq_count, SPAN_ROWS, width),
            precision=lax.Precision.HIGHEST,
        ).reshape(row_count, width)

    d_proj_low = (
        jnp.stack([spread(d_queries), d_keys, d_values], axis=1)
        .astype(jnp.bfloat16)
        .reshape(row_count, 3 * head_cols)
    )
    grad_qkv = outer_sum(tokens_in, d_proj_low).reshape(model_width, 3, head_cols)
    d_entry_part = jnp.einsum("tc,dc->td", d_proj_low, qkv_low, preferred_element_type=jnp.float32)
    input_grad = lax.psum(d_entry_part, "tensor") + spread(d_res_one)
    first_rank = (tensor_slot == 0).astype(jnp.float32)
    width_zero = jnp.zeros((model_width,), jnp.float32)

    def place_heads(partial_sum):
        return lax.dynamic_update_slice_in_dim(width_zero, partial_sum, tensor_slot * head_cols, 0)

    grad_gains = jnp.stack([d_gain_one, d_gain_two]) * first_rank
    grad_biases = jnp.stack(
        [
            place_heads(jnp.sum(d_queries, axis=0)),
            place_heads(jnp.sum(d_values, axis=0)),
            jnp.sum(d_res_one, axis=0) * first_rank,
            d_shift_one * first_rank,
            jnp.sum(d_res_two, axis=0) * first_rank,
            d_shift_two * first_rank,
        ]
    )
    grad_bias_in = lax.dynamic_update_slice_in_dim(
        jnp.zeros(bias_in.shape, jnp.float32), jnp.sum(d_pre, axis=0), tensor_slot * hidden_cols, 0
    )
    grad_gains, grad_biases, grad_bias_in = lax.psum(
        (grad_gains, grad_biases, grad_bias_in), ("dp", "tensor")
    )
    data_slot = lax.axis_index("dp")
    shard_rows = model_width // lax.axis_size("dp")
    owned = tuple(
        (
            lax.psum_scatter(part, "dp", scatter_dimension=0, tiled=True)
            for part in (grad_qkv, grad_out_proj, grad_in, grad_back)
        )
    )
    clock = step[0].astype(jnp.float32)
    warm = warmup[0].astype(jnp.float32)
    horizon = total[0].astype(jnp.float32)
    ratio = jnp.minimum(clock / warm, (horizon - clock) / (horizon - warm))
    corr_one = 1.0 - jnp.power(BETA_ONE, clock)
    corr_two = 1.0 - jnp.power(BETA_TWO, clock)
    change_rows = []
    fresh_moments = []
    for weight, grad_rows, moment in zip(
        (w_qkv, w_out, w_in, w_back), owned, (mom_qkv, mom_out, mom_in, mom_back)
    ):
        weight_rows = lax.dynamic_slice_in_dim(weight, data_slot * shard_rows, shard_rows, 0)
        row_change, new_moment = adam_step(
            weight_rows, grad_rows, moment, ratio, corr_one, corr_two, WEIGHT_DECAY
        )
        change_rows.append(row_change)
        fresh_moments.append(new_moment)
    change_qkv, change_out_proj, change_in_proj, change_back_proj = (
        lax.all_gather(change_rows[0], "dp", axis=0, tiled=True),
        lax.all_gather(change_rows[1], "dp", axis=0, tiled=True),
        lax.all_gather(change_rows[2], "dp", axis=0, tiled=True),
        lax.all_gather(change_rows[3], "dp", axis=0, tiled=True),
    )
    change_gains, new_mom_gains = adam_step(
        gains, grad_gains, mom_gains, ratio, corr_one, corr_two, 0.0
    )
    change_biases, new_mom_biases = adam_step(
        biases, grad_biases, mom_biases, ratio, corr_one, corr_two, 0.0
    )
    change_bias_in, new_mom_bias_in = adam_step(
        bias_in, grad_bias_in, mom_bias_in, ratio, corr_one, corr_two, 0.0
    )
    return (
        normed_out,
        input_grad,
        change_qkv,
        change_out_proj,
        change_in_proj,
        change_back_proj,
        change_gains,
        change_biases,
        change_bias_in,
        fresh_moments[0],
        fresh_moments[1],
        fresh_moments[2],
        fresh_moments[3],
        new_mom_gains,
        new_mom_biases,
        new_mom_bias_in,
    )


def solution(mesh):
    in_specs = (
        P("dp", None),
        P("dp", None),
        P("dp"),
        P("dp"),
        P(),
        P(),
        P(),
        P(None, None, "tensor"),
        P(None, "tensor"),
        P(None, "tensor"),
        P(None, "tensor"),
        P(),
        P(),
        P(),
        P(None, "dp", None, "tensor"),
        P(None, "dp", "tensor"),
        P(None, "dp", "tensor"),
        P(None, "dp", "tensor"),
        P(),
        P(),
        P(),
    )
    out_specs = (
        P("dp", None),
        P("dp", None),
        P(None, None, "tensor"),
        P(None, "tensor"),
        P(None, "tensor"),
        P(None, "tensor"),
        P(),
        P(),
        P(),
        P(None, "dp", None, "tensor"),
        P(None, "dp", "tensor"),
        P(None, "dp", "tensor"),
        P(None, "dp", "tensor"),
        P(),
        P(),
        P(),
    )
    return jax.shard_map(
        on_device, mesh=mesh, in_specs=in_specs, out_specs=out_specs, check_vma=False
    )
```

profile of v0, /device:TPU:0, one launch (start us, length us, event | category | flops | bytes accessed | tf_op | source)
XLA Modules:
  0.0 894.0 jit_solution(5073173420024962855)
XLA Ops:
  7.2 3.9 fusion.15
  34.5 5.7 fusion.20
  41.2 3.0 fusion.96
  46.6 94.5 %all-reduce.6.cloned.1.call-done = f32[1536,768]{1,0:T(8,128)} async-done(((f32[1536,768]{1,0:T(8,128)}), f32[1536,768]{1,0:T(8,128)}) %all-reduce.6.cloned.1.call-update) | async-done | bytes 4718608 | tf_op jit(solution)/shard_map/psum | solution.py:103
  141.1 3.8 fusion.167
  149.2 17.8 %fusion.18 = f32[1536,768]{1,0:T(8,128)} fusion(bf16[1536,768]{1,0:T(8,128)(2,1)} %fusion.14, f32[768]{0:T(1024)} %dynamic_slice.23, f32[768,768]{1,0:T(8,128)} %param.31, f32[768,768]{1,0:T(8,128)} %param.30), kind=kOutput, calls=%fused_computation.39 | convolution fusion | flops 3702915072 | bytes 11799552 | tf_op jit(solution)/shard_map/tf,df->td/dot_general | solution.py:109
  172.6 3.1 fusion.175
  175.7 4.6 fusion.173
  183.3 78.0 %all-reduce.8.cloned.1.call-done = f32[1536,768]{1,0:T(8,128)} async-done(((f32[1536,768]{1,0:T(8,128)}), f32[1536,768]{1,0:T(8,128)}) %all-reduce.8.cloned.1.call-update) | async-done | bytes 4718608 | tf_op jit(solution)/shard_map/psum | solution.py:110
  261.3 5.3 fusion.166
  276.3 4.8 fusion.180
  283.3 33.8 %all-reduce.10.cloned.1.call-done = f32[240,768]{1,0:T(8,128)} async-done(((f32[240,768]{1,0:T(8,128)}), f32[240,768]{1,0:T(8,128)}) %all-reduce.10.cloned.1.call-update) | async-done | bytes 737296 | tf_op jit(solution)/shard_map/psum | solution.py:154
  339.3 4.4 fusion.181
  343.7 3.0 copy.97
  348.8 4.6 fusion.62
  355.3 6.1 convolution_bitcast_fusion
  365.0 51.3 %reduce-scatter.5.cloned.1.call-done = f32[96,3,192]{2,0,1:T(8,128)} async-done(((f32[768,3,192]{2,0,1:T(8,128)}), f32[96,3,192]{2,0,1:T(8,128)}) %reduce-scatter.5.cloned.1.call-update) | async-done | bytes 221200 | tf_op jit(solution)/shard_map/reduce_scatter | solution.py:230
  418.5 69.8 %reduce-scatter.9.cloned.1.call-done = f32[96,768]{1,0:T(8,128)} async-done(((f32[768,768]{1,0:T(8,128)}), f32[96,768]{1,0:T(8,128)}) %reduce-scatter.9.cloned.1.call-update) | async-done | bytes 294928 | tf_op jit(solution)/shard_map/reduce_scatter | solution.py:230
  492.8 3.0 multiply_reduce_fusion
  495.9 4.2 add_convert_fusion
  500.1 59.7 %reduce-scatter.11.cloned.1.call-done = f32[96,768]{1,0:T(8,128)} async-done(((f32[768,768]{1,0:T(8,128)}), f32[96,768]{1,0:T(8,128)}) %reduce-scatter.11.cloned.1.call-update) | async-done | bytes 294928 | tf_op jit(solution)/shard_map/reduce_scatter | solution.py:230
  562.9 40.3 %all-reduce = (f32[2,768]{1,0:T(2,128)S(1)}, f32[6,768]{1,0:T(8,128)S(1)}, f32[3072]{0:T(1024)S(1)}) all-reduce(f32[2,768]{1,0:T(2,128)S(1)} %maximum_multiply_fusion, f32[6,768]{1,0:T(8,128)S(1)} %stack.88, f32[3072]{0:T(1024)S(1)} %dynamic_update_slice.13), channel_id=1, replica_groups=mesh['dp'=8,'tensor'=4] {'dp','tensor'}, use_global_device_ids=true, to_apply=%region_27.28 | all-reduce | flops 9216 | bytes 73728 | tf_op jit(solution)/shard_map/psum | solution.py:223
  607.0 4.3 fusion.47
  611.3 13.9 %reduce-scatter.7.cloned.1.call-done = f32[96,192]{1,0:T(8,128)} async-done(((f32[768,192]{1,0:T(8,128)}), f32[96,192]{1,0:T(8,128)}) %reduce-scatter.7.cloned.1.call-update) | async-done | bytes 73744 | tf_op jit(solution)/shard_map/reduce_scatter | solution.py:230
  626.3 32.2 %all_gather.13 = f32[768,192]{1,0:T(8,128)S(1)} all-gather(f32[96,192]{1,0:T(8,128)S(1)} %get-tuple-element.107), channel_id=1, replica_groups=mesh['dp'=8,'tensor'=4] {'dp'}, dimensions={0}, use_global_device_ids=true | all-gather | bytes 663552 | tf_op jit(solution)/shard_map/all_gather | solution.py:253
  660.3 60.5 %all-reduce.12.cloned.1.call-done = f32[1536,768]{1,0:T(8,128)} async-done(((f32[1536,768]{1,0:T(8,128)}), f32[1536,768]{1,0:T(8,128)}) %all-reduce.12.cloned.1.call-update) | async-done | bytes 4718608 | tf_op jit(solution)/shard_map/psum | solution.py:202
  720.8 6.6 bitcast_add_fusion
  729.9 46.0 %all-gather.4.cloned.1.call-done = f32[768,3,192]{2,0,1:T(8,128)} async-done(((f32[96,3,192]{2,0,1:T(8,128)}), f32[768,3,192]{2,0,1:T(8,128)}) %all-gather.4.cloned.1.call-update) | async-done | bytes 1769488 | tf_op jit(solution)/shard_map/all_gather | solution.py:252
  775.9 2.9 copy.102
  778.8 50.6 %all-gather.6.cloned.1.call-done = f32[768,768]{1,0:T(8,128)} async-done(((f32[96,768]{1,0:T(8,128)}), f32[768,768]{1,0:T(8,128)}) %all-gather.6.cloned.1.call-update) | async-done | bytes 2359312 | tf_op jit(solution)/shard_map/all_gather | solution.py:254
  829.4 53.1 %all-gather.8.cloned.1.call-done = f32[768,768]{1,0:T(8,128)} async-done(((f32[96,768]{1,0:T(8,128)}), f32[768,768]{1,0:T(8,128)}) %all-gather.8.cloned.1.call-update) | async-done | bytes 2359312 | tf_op jit(solution)/shard_map/all_gather | solution.py:255
  882.5 3.4 copy.181
  (269 shorter events, 98.9 us)
Async XLA Ops:
  7.2 263.8 %copy-start = (bf16[1536,768]{1,0:T(8,128)(2,1)S(1)}, bf16[1536,768]{1,0:T(8,128)(2,1)}, u32[]{:S(2)}) copy-start(bf16[1536,768]{1,0:T(8,128)(2,1)} %param.22) | copy-start | bytes 7077892
  7.2 133.9 %all-reduce.6.cloned.1.call-start = ((), (), s32[]{:S(2)}) async-start(), calls=%async_computation.4 | async-start | bytes 9437184 | tf_op jit(solution)/shard_map/psum | solution.py:103
  44.2 217.1 %all-reduce.8.cloned.1.call-start = ((), (), s32[]{:S(2)}) async-start(), calls=%async_computation.5 | async-start | bytes 9437184 | tf_op jit(solution)/shard_map/psum | solution.py:110
  167.0 150.0 %all-reduce.10.cloned.1.call-start = ((), (), s32[]{:S(2)}) async-start(), calls=%async_computation.6 | async-start | bytes 1474560 | tf_op jit(solution)/shard_map/psum | solution.py:154
  180.3 81.0 %copy-start.31 = (f32[1536]{0:T(1024)S(1)}, f32[1536]{0:T(1024)}, u32[]{:S(2)}) copy-start(f32[1536]{0:T(1024)} %copy-done.30) | copy-start | bytes 18436
  180.3 81.0 %copy-start.35 = (f32[1536]{0:T(1024)S(1)}, f32[1536]{0:T(1024)}, u32[]{:S(2)}) copy-start(f32[1536]{0:T(1024)} %copy-done.34) | copy-start | bytes 18436
  180.3 81.0 %copy-start.40 = (f32[768]{0:T(1024)S(1)}, f32[768]{0:T(1024)}, u32[]{:S(2)}) copy-start(f32[768]{0:T(1024)} %get-tuple-element.118) | copy-start | bytes 9220
  180.3 81.0 %copy-start.57 = (f32[768]{0:T(1024)S(1)}, f32[768]{0:T(1024)}, u32[]{:S(2)}) copy-start(f32[768]{0:T(1024)} %get-tuple-element.119) | copy-start | bytes 9220
  282.5 133.8 %reduce-scatter.5.cloned.1.call-start = ((), (), s32[]{:S(2)}) async-start(), calls=%async_computation.8 | async-start | bytes 2654208 | tf_op jit(solution)/shard_map/reduce_scatter | solution.py:230
  346.7 141.6 %reduce-scatter.9.cloned.1.call-start = ((), (), s32[]{:S(2)}) async-start(), calls=%async_computation.11 | async-start | bytes 2654208 | tf_op jit(solution)/shard_map/reduce_scatter | solution.py:230
  348.8 211.1 %reduce-scatter.11.cloned.1.call-start = ((), (), s32[]{:S(2)}) async-start(), calls=%async_computation.13 | async-start | bytes 2654208 | tf_op jit(solution)/shard_map/reduce_scatter | solution.py:230
  353.4 271.8 %reduce-scatter.7.cloned.1.call-start = ((), (), s32[]{:S(2)}) async-start(), calls=%async_computation.10 | async-start | bytes 884736 | tf_op jit(solution)/shard_map/reduce_scatter | solution.py:230
  355.0 365.8 %all-reduce.12.cloned.1.call-start = ((), (), s32[]{:S(2)}) async-start(), calls=%async_computation.7 | async-start | bytes 9437184 | tf_op jit(solution)/shard_map/psum | solution.py:202
  361.3 130.4 %copy-start.38 = (f32[2,6,768]{2,0,1:T(2,128)S(1)}, f32[2,6,768]{2,0,1:T(2,128)}, u32[]{:S(2)}) copy-start(f32[2,6,768]{2,0,1:T(2,128)} %param.40) | copy-start | bytes 110596
  361.3 130.4 %copy-start.42 = (f32[2,3072]{1,0:T(2,128)S(1)}, f32[2,3072]{1,0:T(2,128)}, u32[]{:S(2)}) copy-start(f32[2,3072]{1,0:T(2,128)} %param.41) | copy-start | bytes 73732
  361.3 131.0 %copy-start.7 = (f32[3,80,768]{2,1,0:T(8,128)S(1)}, f32[3,80,768]{2,1,0:T(8,128)}, u32[]{:S(2)}) copy-start(f32[3,80,768]{2,1,0:T(8,128)} %get-tuple-element.137) | copy-start | bytes 2211844
  361.3 131.0 %copy-start.46 = (f32[3,80]{1,0:T(4,128)S(1)}, f32[3,80]{1,0:T(4,128)}, u32[]{:S(2)}) copy-start(f32[3,80]{1,0:T(4,128)} %copy-done.45) | copy-start | bytes 2884
  361.3 131.0 %copy-start.48 = (f32[3,80]{1,0:T(4,128)S(1)}, f32[3,80]{1,0:T(4,128)}, u32[]{:S(2)}) copy-start(f32[3,80]{1,0:T(4,128)} %copy-done.47) | copy-start | bytes 2884
  361.3 131.0 %copy-start.50 = (f32[3,80]{1,0:T(4,128)S(1)}, f32[3,80]{1,0:T(4,128)}, u32[]{:S(2)}) copy-start(f32[3,80]{1,0:T(4,128)} %copy-done.49) | copy-start | bytes 2884
  361.4 131.4 %copy-start.41 = (f32[1536]{0:T(1024)S(1)}, f32[1536]{0:T(1024)}, u32[]{:S(2)}) copy-start(f32[1536]{0:T(1024)} %get-tuple-element.88) | copy-start | bytes 18436
  361.4 414.5 %all-gather.4.cloned.1.call-start = ((), (), s32[]{:S(2)}) async-start(), calls=%async_computation.9 | async-start | bytes 2654208 | tf_op jit(solution)/shard_map/all_gather | solution.py:252
  418.4 77.3 %copy-start.51 = (f32[768]{0:T(1024)S(1)}, f32[768]{0:T(1024)}, u32[]{:S(2)}) copy-start(f32[768]{0:T(1024)} %get-tuple-element.120) | copy-start | bytes 9220
  418.5 410.9 %all-gather.6.cloned.1.call-start = ((), (), s32[]{:S(2)}) async-start(), calls=%async_computation.12 | async-start | bytes 2654208 | tf_op jit(solution)/shard_map/all_gather | solution.py:254
  490.5 392.0 %all-gather.8.cloned.1.call-start = ((), (), s32[]{:S(2)}) async-start(), calls=%async_computation.14 | async-start | bytes 2654208 | tf_op jit(solution)/shard_map/all_gather | solution.py:255
  495.8 66.6 %copy-start.53 = (f32[768]{0:T(1024)S(1)}, f32[768]{0:T(1024)}, u32[]{:S(2)}) copy-start(f32[768]{0:T(1024)} %get-tuple-element.71) | copy-start | bytes 9220
  495.9 107.4 %copy-start.33 = (f32[6,768]{1,0:T(8,128)S(1)}, f32[6,768]{1,0:T(8,128)}, u32[]{:S(2)}) copy-start(f32[6,768]{1,0:T(8,128)} %param.33) | copy-start | bytes 55300
  495.9 108.7 %copy-start.43 = (f32[2,768]{1,0:T(2,128)S(1)}, f32[2,768]{1,0:T(2,128)}, u32[]{:S(2)}) copy-start(f32[2,768]{1,0:T(2,128)} %param.32) | copy-start | bytes 18436
  495.9 108.7 %copy-start.58 = (f32[2,2,768]{2,1,0:T(2,128)S(1)}, f32[2,2,768]{2,1,0:T(2,128)}, u32[]{:S(2)}) copy-start(f32[2,2,768]{2,1,0:T(2,128)} %param.39) | copy-start | bytes 36868
  495.9 109.9 %copy-start.36 = (f32[1,3072]{1,0:T(1,128)S(1)}, f32[1,3072]{1,0:T(1,128)}, u32[]{:S(2)}) copy-start(f32[1,3072]{1,0:T(1,128)} %get-tuple-element.113) | copy-start | bytes 36868
  495.9 109.9 %copy-start.37 = (f32[1,3072]{1,0:T(1,128)S(1)}, f32[1,3072]{1,0:T(1,128)}, u32[]{:S(2)}) copy-start(f32[1,3072]{1,0:T(1,128)} %get-tuple-element.114) | copy-start | bytes 36868
  495.9 109.9 %copy-start.44 = (f32[3072]{0:T(1024)S(1)}, f32[3072]{0:T(1024)}, u32[]{:S(2)}) copy-start(f32[3072]{0:T(1024)} %param.34) | copy-start | bytes 36868
  660.3 67.1 %copy-start.25 = (f32[1,96,3,192]{3,1,2,0:T(8,128)S(1)}, f32[1,96,3,192]{3,1,2,0:T(8,128)}, u32[]{:S(2)}) copy-start(f32[1,96,3,192]{3,1,2,0:T(8,128)} %get-tuple-element.103) | copy-start | bytes 663556
  (43 other events, 607.0 us)
Sparse Core Ops, SparseCore 0:
  44.3 96.7 all-reduce.5
  167.1 94.1 all-reduce.7
  282.6 34.3 all-reduce.9
  346.9 69.3 reduce-scatter.4
  420.2 68.0 reduce-scatter.8
  491.6 68.1 reduce-scatter.10
  563.7 61.4 reduce-scatter.6
  627.8 92.9 all-reduce.11
  723.8 52.0 all-gather.3
  778.8 50.5 all-gather.5
  831.8 50.5 all-gather.7
where the time goes:
time: 903 us; the launch traced here: 894 us
  waiting for transfers between devices  611 us (68%)
  matrix products  86.9 us (10%)
  blocking collectives  72.5 us (8%)
  other arithmetic  56.1 us (6%)
  local copies, waits for them, and re-layouts  48.5 us (5%)
  between operations  17.2 us (2%)
    reduce_scatter x4, waiting for transfers between devices, on_device(): lax.psum_scatter(part, 'dp', scatter_dimension=0, tiled=True)  195 us
    psum x1, waiting for transfers between devices, on_device(): attn_sum = lax.psum(attn_part, 'tensor')  94.5 us
    psum x1, waiting for transfers between devices, on_device(): down_sum = lax.psum(down_part, 'tensor')  78 us
    psum x1, waiting for transfers between devices, on_device(): input_grad = lax.psum(d_entry_part, 'tensor') + spread(d_res_one)  60.5 us
    all_gather x1, waiting for transfers between devices, on_device(): lax.all_gather(change_rows[3], 'dp', axis=0, tiled=True)  53.1 us
    all_gather x1, waiting for transfers between devices, on_device(): lax.all_gather(change_rows[2], 'dp', axis=0, tiled=True)  50.6 us
    all_gather x1, waiting for transfers between devices, on_device(): lax.all_gather(change_rows[0], 'dp', axis=0, tiled=True)  46 us
    psum x1, blocking collectives, on_device(): lax.psum((grad_gains, grad_biases, grad_bias_in), ('dp', 'tensor'))  40.3 us
  transfers between devices with their start and end apart: 11, of which 11 were waited for; matrix products, arithmetic and copies ran while one was open for 8% of the time, Pallas kernels for 0%

commit v1 on v0

--- a/solution.py
+++ b/solution.py
@@ -11,6 +11,28 @@
 BETA_TWO = 0.999
 ADAM_EPS = 1e-06
 WEIGHT_DECAY = 0.01
+
+
+def laid_out(blocks, dim):
+    shape = list(blocks.shape[1:])
+    shape[dim] *= blocks.shape[0]
+    return jnp.moveaxis(blocks, 0, dim).reshape(shape)
+
+
+def collect(x, axis, dim):
+    size = lax.axis_size(axis)
+    pairs = [(i, (i + 1) % size) for i in range(size)]
+    back = [(b, a) for a, b in pairs]
+    lower, upper = ([], [])
+    for step in range(size - 1):
+        if step % 2 == 0:
+            lower.append(lax.ppermute(lower[-1] if lower else x, axis, pairs))
+        else:
+            upper.append(lax.ppermute(upper[-1] if upper else x, axis, back))
+    blocks = jnp.stack([*lower[::-1], x, *upper])
+    shift = lax.axis_index(axis) - len(lower)
+    blocks = blocks[(jnp.arange(size) - shift) % size]
+    return laid_out(blocks, dim)
 
 
 def layer_norm(values, gain, shift):
@@ -249,7 +271,7 @@
         change_rows.append(row_change)
         fresh_moments.append(new_moment)
     change_qkv, change_out_proj, change_in_proj, change_back_proj = (
-        lax.all_gather(change_rows[0], "dp", axis=0, tiled=True),
+        collect(change_rows[0], "dp", 0),
         lax.all_gather(change_rows[1], "dp", axis=0, tiled=True),
         lax.all_gather(change_rows[2], "dp", axis=0, tiled=True),
         lax.all_gather(change_rows[3], "dp", axis=0, tiled=True),

time: 903 us -> 833 us (0.922)
  waiting for transfers between devices: 611 us -> 512 us
  local copies, waits for them, and re-layouts: 48.5 us -> 61.8 us
  starting transfers between devices: 1.42 us -> 11.4 us
    all_gather x1 -> x0, waiting for transfers between devices: 46 us -> none  [on_device(): lax.all_gather(change_rows[0], 'dp', axis=0, tiled=True)]
    all_gather x1, waiting for transfers between devices: 50.6 us -> 20.2 us  [on_device(): lax.all_gather(change_rows[2], 'dp', axis=0, tiled=True)]
    psum x1, waiting for transfers between devices: 33.8 us -> 15.6 us  [on_device(): d_normed = lax.psum(d_normed_part, 'tensor') + d_res_two]
    reduce_scatter x4, waiting for transfers between devices: 195 us -> 177 us  [on_device(): lax.psum_scatter(part, 'dp', scatter_dimension=0, tiled=True)]
    ppermute x0 -> x7, waiting for transfers between devices: none -> 14.1 us  [the longest x4 14.1 us: collect(): lower.append(lax.ppermute(lower[-1] if lower else x, axis, pairs))]
    psum x1, waiting for transfers between devices: 60.5 us -> 47.6 us  [on_device(): input_grad = lax.psum(d_entry_part, 'tensor') + spread(d_res_one)]
    psum x1, waiting for transfers between devices: 78 us -> 88.2 us  [on_device(): down_sum = lax.psum(down_part, 'tensor')]
    ppermute x0 -> x7, starting transfers between devices: none -> 10 us  [the longest x3 8.55 us: collect(): upper.append(lax.ppermute(upper[-1] if upper else x, axis, back))]
  transfers between devices with their start and end apart: 11 -> 17, of which waited for: 11 -> 11; matrix products, arithmetic and copies ran while one was open for 8% -> 13% of each run, Pallas kernels for 0% -> 0%
where the time goes in v1:
time: 833 us; the launch traced here: 824 us
  waiting for transfers between devices  512 us (61%)
  matrix products  88.8 us (11%)
  blocking collectives  80.9 us (10%)
  local copies, waits for them, and re-layouts  61.8 us (7%)
  other arithmetic  52.1 us (6%)
  between operations  17.3 us (2%)
  starting transfers between devices  11.4 us (1%)
    reduce_scatter x4, waiting for transfers between devices, on_device(): lax.psum_scatter(part, 'dp', scatter_dimension=0, tiled=True)  177 us
    psum x1, waiting for transfers between devices, on_device(): attn_sum = lax.psum(attn_part, 'tensor')  96.1 us
    psum x1, waiting for transfers between devices, on_device(): down_sum = lax.psum(down_part, 'tensor')  88.2 us
    all_gather x1, waiting for transfers between devices, on_device(): lax.all_gather(change_rows[3], 'dp', axis=0, tiled=True)  52.9 us
    psum x1, waiting for transfers between devices, on_device(): input_grad = lax.psum(d_entry_part, 'tensor') + spread(d_res_one)  47.6 us
    psum x1, blocking collectives, on_device(): lax.psum((grad_gains, grad_biases, grad_bias_in), ('dp', 'tensor'))  40.8 us
    all_gather x1, blocking collectives, on_device(): lax.all_gather(change_rows[1], 'dp', axis=0, tiled=True)  40.1 us
    unnamed x90, local copies, waits for them, and re-layouts  22.3 us
  transfers between devices with their start and end apart: 17, of which 11 were waited for; matrix products, arithmetic and copies ran while one was open for 13% of the time, Pallas kernels for 0%

profile of v1, /device:TPU:0, one launch (start us, length us, event | category | flops | bytes accessed | tf_op | source)
XLA Modules:
  0.0 824.3 jit_solution(11945936480373938057)
XLA Ops:
  7.2 3.9 fusion.15
  36.0 5.7 fusion.20
  42.7 3.0 fusion.96
  46.6 96.1 %all-reduce.6.cloned.1.call-done = f32[1536,768]{1,0:T(8,128)} async-done(((f32[1536,768]{1,0:T(8,128)}), f32[1536,768]{1,0:T(8,128)}) %all-reduce.6.cloned.1.call-update) | async-done | bytes 4718608 | tf_op jit(solution)/shard_map/psum | solution.py:125
  142.6 3.8 fusion.169
  150.6 17.8 %fusion.18 = f32[1536,768]{1,0:T(8,128)} fusion(bf16[1536,768]{1,0:T(8,128)(2,1)} %fusion.14, f32[768]{0:T(1024)S(1)} %dynamic_slice.23, f32[768,768]{1,0:T(8,128)} %param.31, f32[768,768]{1,0:T(8,128)} %param.30), kind=kOutput, calls=%fused_computation.40 | convolution fusion | flops 3702915072 | bytes 11799552 | tf_op jit(solution)/shard_map/tf,df->td/dot_general | solution.py:131
  171.6 3.0 convolution_add_fusion.1
  174.6 88.2 %all-reduce.8.cloned.1.call-done = f32[1536,768]{1,0:T(8,128)} async-done(((f32[1536,768]{1,0:T(8,128)}), f32[1536,768]{1,0:T(8,128)}) %all-reduce.8.cloned.1.call-update) | async-done | bytes 4718608 | tf_op jit(solution)/shard_map/psum | solution.py:132
  262.8 4.7 fusion.168
  277.1 4.8 fusion.182
  284.1 3.0 fusion.89
  292.9 4.5 fusion.175
  297.4 4.6 fusion.62
  303.0 15.6 %all-reduce.10.cloned.1.call-done = f32[240,768]{1,0:T(8,128)} async-done(((f32[240,768]{1,0:T(8,128)}), f32[240,768]{1,0:T(8,128)}) %all-reduce.10.cloned.1.call-update) | async-done | bytes 737296 | tf_op jit(solution)/shard_map/psum | solution.py:176
  339.4 4.4 fusion.183
  343.8 3.0 copy.96
  348.5 6.1 convolution_bitcast_fusion
  360.5 31.2 %reduce-scatter.9.cloned.1.call-done = f32[96,768]{1,0:T(8,128)} async-done(((f32[768,768]{1,0:T(8,128)}), f32[96,768]{1,0:T(8,128)}) %reduce-scatter.9.cloned.1.call-update) | async-done | bytes 294928 | tf_op jit(solution)/shard_map/reduce_scatter | solution.py:252
  397.5 3.9 add_convert_fusion
  402.1 40.8 %all-reduce = (f32[2,768]{1,0:T(2,128)S(1)}, f32[6,768]{1,0:T(8,128)S(1)}, f32[3072]{0:T(1024)S(1)}) all-reduce(f32[2,768]{1,0:T(2,128)S(1)} %maximum_multiply_fusion, f32[6,768]{1,0:T(8,128)S(1)} %stack.124, f32[3072]{0:T(1024)S(1)} %dynamic_update_slice.13), channel_id=1, replica_groups=mesh['dp'=8,'tensor'=4] {'dp','tensor'}, use_global_device_ids=true, to_apply=%region_27.28 | all-reduce | flops 9216 | bytes 73728 | tf_op jit(solution)/shard_map/psum | solution.py:245
  445.4 4.3 fusion.47
  449.7 13.9 %reduce-scatter.11.cloned.1.call-done = f32[96,768]{1,0:T(8,128)} async-done(((f32[768,768]{1,0:T(8,128)}), f32[96,768]{1,0:T(8,128)}) %reduce-scatter.11.cloned.1.call-update) | async-done | bytes 294928 | tf_op jit(solution)/shard_map/reduce_scatter | solution.py:252
  466.9 68.7 %reduce-scatter.5.cloned.1.call-done = f32[96,3,192]{2,0,1:T(8,128)} async-done(((f32[768,3,192]{2,0,1:T(8,128)}), f32[96,3,192]{2,0,1:T(8,128)}) %reduce-scatter.5.cloned.1.call-update) | async-done | bytes 221200 | tf_op jit(solution)/shard_map/reduce_scatter | solution.py:252
  537.8 63.3 %reduce-scatter.7.cloned.1.call-done = f32[96,192]{1,0:T(8,128)} async-done(((f32[768,192]{1,0:T(8,128)}), f32[96,192]{1,0:T(8,128)}) %reduce-scatter.7.cloned.1.call-update) | async-done | bytes 73744 | tf_op jit(solution)/shard_map/reduce_scatter | solution.py:252
  604.5 40.1 %all_gather.9 = f32[768,192]{1,0:T(8,128)S(1)} all-gather(f32[96,192]{1,0:T(8,128)S(1)} %get-tuple-element.107), channel_id=1, replica_groups=mesh['dp'=8,'tensor'=4] {'dp'}, dimensions={0}, use_global_device_ids=true | all-gather | bytes 663552 | tf_op jit(solution)/shard_map/all_gather | solution.py:275
  649.0 47.6 %all-reduce.12.cloned.1.call-done = f32[1536,768]{1,0:T(8,128)} async-done(((f32[1536,768]{1,0:T(8,128)}), f32[1536,768]{1,0:T(8,128)}) %all-reduce.12.cloned.1.call-update) | async-done | bytes 4718608 | tf_op jit(solution)/shard_map/psum | solution.py:224
  696.6 6.6 bitcast_add_fusion
  704.1 4.2 collective-permute-start.6
  710.0 14.1 %collective-permute-done.3 = f32[96,3,192]{2,0,1:T(8,128)S(1)} collective-permute-done((f32[96,3,192]{2,0,1:T(8,128)S(1)}, f32[96,3,192]{2,0,1:T(8,128)S(1)}, u32[]{:S(2)}, u32[]{:S(2)}) %collective-permute-start.3) | collective-permute-done | bytes 221216 | tf_op jit(solution)/shard_map/ppermute | solution.py:29
  739.4 20.2 %all-gather.3.cloned.1.call-done = f32[768,768]{1,0:T(8,128)} async-done(((f32[96,768]{1,0:T(8,128)}), f32[768,768]{1,0:T(8,128)}) %all-gather.3.cloned.1.call-update) | async-done | bytes 2359312 | tf_op jit(solution)/shard_map/all_gather | solution.py:276
  759.6 52.9 %all-gather.5.cloned.1.call-done = f32[768,768]{1,0:T(8,128)} async-done(((f32[96,768]{1,0:T(8,128)}), f32[768,768]{1,0:T(8,128)}) %all-gather.5.cloned.1.call-update) | async-done | bytes 2359312 | tf_op jit(solution)/shard_map/all_gather | solution.py:277
  812.5 3.4 copy.187
  (240 shorter events, 119.6 us)
Async XLA Ops:
  7.2 264.7 %copy-start = (bf16[1536,768]{1,0:T(8,128)(2,1)S(1)}, bf16[1536,768]{1,0:T(8,128)(2,1)}, u32[]{:S(2)}) copy-start(bf16[1536,768]{1,0:T(8,128)(2,1)} %param.22) | copy-start | bytes 7077892
  7.2 135.4 %all-reduce.6.cloned.1.call-start = ((), (), s32[]{:S(2)}) async-start(), calls=%async_computation.4 | async-start | bytes 9437184 | tf_op jit(solution)/shard_map/psum | solution.py:125
  13.2 14.2 %copy-start.7 = (f32[1536,1,192]{0,2,1:T(8,128)}, f32[1536,1,192]{0,2,1:T(8,128)S(1)}, u32[]{:S(2)}) copy-start(f32[1536,1,192]{0,2,1:T(8,128)S(1)} %get-tuple-element.95) | copy-start | bytes 3538948
  36.0 5.7 copy-start.14
  36.0 6.7 copy-start.18
  45.7 96.9 %copy-start.29 = (f32[768]{0:T(1024)S(1)}, f32[768]{0:T(1024)}, u32[]{:S(2)}) copy-start(f32[768]{0:T(1024)} %get-tuple-element.117) | copy-start | bytes 9220
  45.8 217.0 %all-reduce.8.cloned.1.call-start = ((), (), s32[]{:S(2)}) async-start(), calls=%async_computation.5 | async-start | bytes 9437184 | tf_op jit(solution)/shard_map/psum | solution.py:132
  168.4 94.4 %copy-start.31 = (f32[768]{0:T(1024)S(1)}, f32[768]{0:T(1024)}, u32[]{:S(2)}) copy-start(f32[768]{0:T(1024)} %get-tuple-element.119) | copy-start | bytes 9220
  168.4 150.1 %all-reduce.10.cloned.1.call-start = ((), (), s32[]{:S(2)}) async-start(), calls=%async_computation.6 | async-start | bytes 1474560 | tf_op jit(solution)/shard_map/psum | solution.py:176
  284.1 7.0 copy-start.10
  284.1 107.6 %reduce-scatter.9.cloned.1.call-start = ((), (), s32[]{:S(2)}) async-start(), calls=%async_computation.10 | async-start | bytes 2654208 | tf_op jit(solution)/shard_map/reduce_scatter | solution.py:252
  287.2 176.4 %reduce-scatter.11.cloned.1.call-start = ((), (), s32[]{:S(2)}) async-start(), calls=%async_computation.12 | async-start | bytes 2654208 | tf_op jit(solution)/shard_map/reduce_scatter | solution.py:252
  289.0 8.3 %copy-start.16 = (f32[240,768]{1,0:T(8,128)S(1)}, f32[240,768]{1,0:T(8,128)}, u32[]{:S(2)}) copy-start(f32[240,768]{1,0:T(8,128)} %copy-done.15) | copy-start | bytes 2211844
  301.9 233.7 %reduce-scatter.5.cloned.1.call-start = ((), (), s32[]{:S(2)}) async-start(), calls=%async_computation.8 | async-start | bytes 2654208 | tf_op jit(solution)/shard_map/reduce_scatter | solution.py:252
  320.8 7.4 copy-start.9
  331.1 6.9 copy-start.20
  346.9 254.2 %reduce-scatter.7.cloned.1.call-start = ((), (), s32[]{:S(2)}) async-start(), calls=%async_computation.9 | async-start | bytes 884736 | tf_op jit(solution)/shard_map/reduce_scatter | solution.py:252
  348.5 348.2 %all-reduce.12.cloned.1.call-start = ((), (), s32[]{:S(2)}) async-start(), calls=%async_computation.7 | async-start | bytes 9437184 | tf_op jit(solution)/shard_map/psum | solution.py:224
  354.6 39.5 %copy-start.30 = (f32[768]{0:T(1024)S(1)}, f32[768]{0:T(1024)}, u32[]{:S(2)}) copy-start(f32[768]{0:T(1024)} %get-tuple-element.70) | copy-start | bytes 9220
  354.6 39.6 %copy-start.34 = (f32[768]{0:T(1024)S(1)}, f32[768]{0:T(1024)}, u32[]{:S(2)}) copy-start(f32[768]{0:T(1024)} %get-tuple-element.146) | copy-start | bytes 9220
  354.7 404.9 %all-gather.3.cloned.1.call-start = ((), (), s32[]{:S(2)}) async-start(), calls=%async_computation.11 | async-start | bytes 2654208 | tf_op jit(solution)/shard_map/all_gather | solution.py:276
  393.9 418.6 %all-gather.5.cloned.1.call-start = ((), (), s32[]{:S(2)}) async-start(), calls=%async_computation.13 | async-start | bytes 2654208 | tf_op jit(solution)/shard_map/all_gather | solution.py:277
  397.5 45.4 %copy-start.24 = (f32[6,768]{1,0:T(8,128)S(1)}, f32[6,768]{1,0:T(8,128)}, u32[]{:S(2)}) copy-start(f32[6,768]{1,0:T(8,128)} %param.33) | copy-start | bytes 55300
  397.5 46.0 %copy-start.32 = (f32[2,2,768]{2,1,0:T(2,128)S(1)}, f32[2,2,768]{2,1,0:T(2,128)}, u32[]{:S(2)}) copy-start(f32[2,2,768]{2,1,0:T(2,128)} %param.39) | copy-start | bytes 36868
  401.4 62.2 %copy-start.22 = (f32[2,96,768]{2,1,0:T(8,128)S(1)}, f32[2,96,768]{2,1,0:T(8,128)}, u32[]{:S(2)}) copy-start(f32[2,96,768]{2,1,0:T(8,128)} %param.38) | copy-start | bytes 1769476
  537.0 67.5 %collective-permute-start = (f32[96,3,192]{2,0,1:T(8,128)S(1)}, f32[96,3,192]{2,0,1:T(8,128)S(1)}, u32[]{:S(2)}, u32[]{:S(2)}) collective-permute-start(f32[96,3,192]{2,0,1:T(8,128)S(1)} %get-tuple-element.104), channel_id=1, source_target_pairs={{0,4},{4,8},{8,12},{12,16},{16,20},{20,24},{24,28},{28,0},{1,5},{5... | collective-permute-start | bytes 663560 | tf_op jit(solution)/shard_map/ppermute | solution.py:29
  602.1 44.2 %collective-permute-start.4 = (f32[96,3,192]{2,0,1:T(8,128)S(1)}, f32[96,3,192]{2,0,1:T(8,128)}, u32[]{:S(2)}, u32[]{:S(2)}) collective-permute-start(f32[96,3,192]{2,0,1:T(8,128)S(1)} %get-tuple-element.104), channel_id=1, source_target_pairs={{4,0},{8,4},{12,8},{16,12},{20,16},{24,20},{28,24},{0,28},{5,1},{9... | collective-permute-start | bytes 663560 | tf_op jit(solution)/shard_map/ppermute | solution.py:31
  604.5 43.9 %collective-permute-start.1 = (f32[96,3,192]{2,0,1:T(8,128)S(1)}, f32[96,3,192]{2,0,1:T(8,128)}, u32[]{:S(2)}, u32[]{:S(2)}) collective-permute-start(f32[96,3,192]{2,0,1:T(8,128)S(1)} %collective-permute-done), channel_id=1, source_target_pairs={{0,4},{4,8},{8,12},{12,16},{16,20},{20,24},{24,28},{28,0},{1,5},{5... | collective-permute-start | bytes 663560 | tf_op jit(solution)/shard_map/ppermute | solution.py:29
  646.4 57.7 %collective-permute-start.5 = (f32[96,3,192]{2,0,1:T(8,128)}, f32[96,3,192]{2,0,1:T(8,128)S(1)}, u32[]{:S(2)}, u32[]{:S(2)}) collective-permute-start(f32[96,3,192]{2,0,1:T(8,128)} %collective-permute-done.4), channel_id=1, source_target_pairs={{4,0},{8,4},{12,8},{16,12},{20,16},{24,20},{28,24},{0,28},{5,1},{9... | collective-permute-start | bytes 663560 | tf_op jit(solution)/shard_map/ppermute | solution.py:31
  648.4 59.9 %collective-permute-start.2 = (f32[96,3,192]{2,0,1:T(8,128)}, f32[96,3,192]{2,0,1:T(8,128)S(1)}, u32[]{:S(2)}, u32[]{:S(2)}) collective-permute-start(f32[96,3,192]{2,0,1:T(8,128)} %collective-permute-done.1), channel_id=1, source_target_pairs={{0,4},{4,8},{8,12},{12,16},{16,20},{20,24},{24,28},{28,0},{1,5},{5... | collective-permute-start | bytes 663560 | tf_op jit(solution)/shard_map/ppermute | solution.py:29
  704.1 27.1 %collective-permute-start.6 = (f32[96,3,192]{2,0,1:T(8,128)S(1)}, f32[96,3,192]{2,0,1:T(8,128)S(1)}, u32[]{:S(2)}, u32[]{:S(2)}) collective-permute-start(f32[96,3,192]{2,0,1:T(8,128)S(1)} %collective-permute-done.5), channel_id=1, source_target_pairs={{4,0},{8,4},{12,8},{16,12},{20,16},{24,20},{28,24},{0,28},{5,1},{9... | collective-permute-start | bytes 663560 | tf_op jit(solution)/shard_map/ppermute | solution.py:31
  708.3 15.8 %collective-permute-start.3 = (f32[96,3,192]{2,0,1:T(8,128)S(1)}, f32[96,3,192]{2,0,1:T(8,128)S(1)}, u32[]{:S(2)}, u32[]{:S(2)}) collective-permute-start(f32[96,3,192]{2,0,1:T(8,128)S(1)} %collective-permute-done.2), channel_id=1, source_target_pairs={{0,4},{4,8},{8,12},{12,16},{16,20},{20,24},{24,28},{28,0},{1,5},{5... | collective-permute-start | bytes 663560 | tf_op jit(solution)/shard_map/ppermute | solution.py:29
  (23 other events, 69.1 us)
Sparse Core Ops, SparseCore 0:
  45.9 96.7 all-reduce.5
  168.6 94.1 all-reduce.7
  284.2 34.3 all-reduce.9
  322.5 69.1 reduce-scatter.8
  395.1 68.5 reduce-scatter.10
  467.5 68.0 reduce-scatter.4
  539.5 61.5 reduce-scatter.6
  603.6 93.0 all-reduce.11
  699.6 59.8 all-gather.2
  761.8 50.6 all-gather.4
